TPU v7x, 32 devices: a whole 2x2x4 slice. The times are simulated.
32 devices in a mesh: leaf: 8 (over z, y), front: 4 (over x, core).
Axes of the slice: x: 2, y: 2, z: 4, core: 2. Of those that a mesh axis runs over, the one named last changes fastest.
Arguments:
- leaf_fronts: float32 [8, 1024, 1024], P('leaf', 'front')
- coupling_cols: int32 [8, 4, 224, 128], P('leaf', 'front'), may hold values from 0 to 1023, as said below
- coupling_vals: float32 [8, 4, 224, 128], P('leaf', 'front'), may hold values from -0.1 to 0.1
- sep_diag: float32 [8, 4, 224], P('leaf', 'front'), may hold values from 1 to 3
- child_maps: int32 [14, 512], replicated, may hold values from 0 to 1023, as said below
Outputs:
- factors: float32 [8, 4, 480, 512], P('leaf', 'front')
- log_det: float32 [], replicated
Inputs may be any that keep to these rules, and one draw needn't show every extreme that they name: `coupling_cols`: each coupling column is at most the index, in its front, of the row that holds it, so every entry lies on or below the diagonal. `child_maps`: the 512 entries of each row are distinct.
All inputs are finite; a program needn't handle non-finite values.
Results may differ from a plain program's by a relative error of at most 0.0001.
Values sent between devices are 32-bit elements; how exact they have to be, the bound alone decides.
No kernel may reach another device: no remote copies, remote signals or barrier semaphores. Data moves between devices by JAX's collectives and lax.ppermute only.
A program may use at most 128 MiB of HBM per device.

v0:
```python
import jax
import jax.numpy as jnp
from jax import lax
from jax.sharding import PartitionSpec as P

SEP = 512
BND = 512


highest_precision = lax.Precision.HIGHEST


def swapped(block, axis, distance):
    count = lax.axis_size(axis)
    route = []
    for low in range(count):
        high = low | 1 << distance
        if high != low and high < count:
            route += [(low, high), (high, low)]
    return lax.ppermute(block, axis, route)


def from_behind(block, axis, distance):
    devices = range(lax.axis_size(axis))
    route = [(i - distance, i) for i in devices if i - distance in devices]
    return lax.ppermute(block, axis, route)


def symmetric_of(lower_tri):
    return lower_tri + lower_tri.T - jnp.diag(jnp.diag(lower_tri))


def double_up(gathered, partner, bit_pos):
    leaf_pos = lax.axis_index("leaf")
    high_side = leaf_pos >> bit_pos & 1 == 1
    first_half = jnp.where(high_side, partner, gathered)
    second_half = jnp.where(high_side, gathered, partner)
    return jnp.concatenate([first_half, second_half], axis=0)


def collect(strip_piece, bit_count, is_panel):
    if is_panel:
        gathered = lax.all_gather(strip_piece, "front", axis=0, tiled=True)
    else:
        gathered = lax.all_gather(strip_piece, "front", axis=0, tiled=True)
    for bit_pos in range(bit_count):
        if is_panel:
            partner = swapped(gathered, "leaf", bit_pos)
        else:
            partner = swapped(gathered, "leaf", bit_pos)
        gathered = double_up(gathered, partner, bit_pos)
    return gathered


def twin_order(gathered, group_size):
    row_count = gathered.shape[0] // (2 * group_size)
    col_count = gathered.shape[1]
    arranged = gathered.reshape(2, 2, group_size // 2, row_count, col_count)
    return arranged.transpose(0, 2, 1, 3, 4).reshape(2, group_size * row_count, col_count)


def child_rows(update_rows, index_map, row_ids):
    match_grid = index_map[None, :] == row_ids[:, None]
    child_ids = jnp.arange(index_map.shape[0], dtype=jnp.int32)
    present = jnp.any(match_grid, axis=1)
    source = jnp.sum(jnp.where(match_grid, child_ids[None, :], 0), axis=1)
    row_part = jnp.take(update_rows, source, axis=0)
    col_part = jnp.take(update_rows, source, axis=1).T
    picked = jnp.where(child_ids[None, :] <= source[:, None], row_part, col_part)
    return jnp.where(present[:, None], picked, 0.0)


def body(leaf_fronts, coupling_cols, coupling_vals, sep_diag, child_maps):
    group_count = lax.axis_size("leaf")
    front_count = lax.axis_size("front")
    level_total = group_count.bit_length()
    width_all = SEP + BND
    leaf_pos = lax.axis_index("leaf")
    front_pos = lax.axis_index("front")
    size_rows = width_all // front_count
    row_ids = front_pos * size_rows + jnp.arange(size_rows, dtype=jnp.int32)
    column_ids = jnp.arange(width_all, dtype=jnp.int32)
    front_strip = jnp.where(column_ids[None, :] <= row_ids[:, None], leaf_fronts[0], 0.0)
    pieces_out = []
    log_part = jnp.zeros((), jnp.float32)
    list_offset = 0
    map_base = 0
    for level_no in range(level_total):
        span_leaf = 1 << level_no
        size_rows = width_all // (front_count * span_leaf)
        group_rank = (leaf_pos & span_leaf - 1) * front_count + front_pos
        start_row = group_rank * size_rows
        panel_piece = front_strip[:, :SEP]
        panel_cols = collect(panel_piece, level_no, True)
        head_block = symmetric_of(panel_cols[:SEP])
        chol_head = jnp.linalg.cholesky(head_block)
        below = jax.scipy.linalg.solve_triangular(chol_head, panel_cols[SEP:].T, lower=True).T
        factor_cols = jnp.concatenate([chol_head, below], axis=0)
        pieces_out.append(lax.dynamic_slice_in_dim(factor_cols, start_row, size_rows, 0))
        head_diag = jnp.diagonal(chol_head)
        owned_rows = jnp.arange(SEP, dtype=jnp.int32) // size_rows == group_rank
        log_part = log_part + jnp.sum(jnp.where(owned_rows, jnp.log(head_diag), 0.0))
        if level_no + 1 < level_total:
            group_size = span_leaf * front_count
            half_rows = size_rows // 2
            holds_tail = group_rank >= group_size // 2
            update_start = start_row - jnp.where(holds_tail, SEP, 0)
            tail_rows = front_strip[:, SEP:]

            def tail_term():
                own_below = lax.dynamic_slice_in_dim(
                    below, jnp.clip(update_start, 0, BND - size_rows), size_rows, 0
                )
                return tail_rows - jnp.dot(
                    own_below,
                    below.T,
                    precision=highest_precision,
                    preferred_element_type=jnp.float32,
                )

            def empty_term():
                return jnp.zeros((size_rows, BND), jnp.float32)

            difference = lax.cond(holds_tail, tail_term, empty_term)
            leading = difference[:half_rows]
            if level_no == 0:
                received = from_behind(leading, "front", -(front_count // 2))
            else:
                received = from_behind(leading, "leaf", -(1 << level_no - 1))
            outgoing = jnp.where(holds_tail, difference[half_rows:], received)
            gathered = twin_order(collect(outgoing, level_no + 1, False), group_size)
            parent_span = span_leaf * 2
            next_rows = width_all // (front_count * parent_span)
            parent_rank = (leaf_pos & parent_span - 1) * front_count + front_pos
            row_ids = parent_rank * next_rows + jnp.arange(next_rows, dtype=jnp.int32)
            parent_no = leaf_pos >> level_no + 1
            assembled = jnp.zeros((next_rows, width_all), jnp.float32)
            for child_no in range(2):
                index_map = lax.dynamic_slice_in_dim(
                    child_maps, map_base + 2 * parent_no + child_no, 1, 0
                )[0]
                picked = child_rows(gathered[child_no], index_map, row_ids)
                assembled = assembled.at[:, index_map].add(picked)
            assembled = jnp.where(column_ids[None, :] <= row_ids[:, None], assembled, 0.0)
            col_block = coupling_cols[0, 0, list_offset : list_offset + next_rows, :]
            val_block = coupling_vals[0, 0, list_offset : list_offset + next_rows, :]
            local_rows = jnp.arange(next_rows, dtype=jnp.int32)
            assembled = assembled.at[local_rows[:, None], col_block].add(val_block)
            diag_piece = sep_diag[0, 0, list_offset : list_offset + next_rows]
            assembled = assembled + jnp.where(
                column_ids[None, :] == row_ids[:, None], diag_piece[:, None], 0.0
            )
            front_strip = assembled
            list_offset = list_offset + next_rows
            map_base = map_base + group_count // span_leaf
    log_det = 2.0 * lax.psum(log_part, ("leaf", "front"))
    factors = jnp.concatenate(pieces_out, axis=0)[None, None]
    return (factors, log_det)


def solution(mesh):
    placed = (
        P("leaf", "front", None),
        P("leaf", "front", None, None),
        P("leaf", "front", None, None),
        P("leaf", "front", None),
        P(),
    )
    return jax.shard_map(
        body,
        mesh=mesh,
        in_specs=placed,
        out_specs=(P("leaf", "front", None, None), P()),
        check_vma=False,
    )
```

profile of v0, /device:TPU:0, one launch (start us, length us, event | category | flops | bytes accessed | tf_op | source)
XLA Modules:
  0.0 1349.4 jit_solution(14997081369363047042)
XLA Ops:
  10.5 25.4 %all-gather.4.cloned.1.call-done = f32[1024,512]{1,0:T(8,128)} async-done(((f32[256,512]{1,0:T(8,128)}), f32[1024,512]{1,0:T(8,128)}) %all-gather.4.cloned.1.call-update) | async-done | bytes 2097168 | tf_op jit(solution)/shard_map/all_gather | solution.py:43
  46.5 11.7 cholesky.462
  68.8 11.7 cholesky.481
  91.5 11.7 cholesky.502
  114.3 11.7 cholesky.519
  131.5 12.0 while.8
  143.5 39.3 %custom-call.54 = f32[4,128,128]{1,2,0:T(8,128)S(1)} custom-call(f32[4,128,128]{2,1,0:T(8,128)S(1)} %get-tuple-element.105), custom_call_target="InvertDiagBlocksLowerTriangular" | custom-call | tf_op jit(solution)/shard_map/jit(_solve_triangular)/triangular_solve | solution.py:97
  214.7 13.3 all-gather.6.cloned.1.call-done
  230.9 22.7 %collective-permute-done.1 = f32[512,512]{1,0:T(8,128)S(1)} collective-permute-done((f32[512,512]{1,0:T(8,128)}, f32[512,512]{1,0:T(8,128)S(1)}, u32[]{:S(2)}, u32[]{:S(2)}) %collective-permute-start.1) | collective-permute-done | bytes 1048608 | tf_op jit(solution)/shard_map/ppermute | solution.py:20
  270.1 113.4 %scatter_fusion.3 = f32[131072]{0:T(1024)S(1)} fusion(f32[131072]{0:T(1024)S(1)} %bitcast.322, s32[16384]{0:T(1024)S(1)} %select_bitcast_fusion.15, f32[16384]{0:T(1024)S(1)} %slice_bitcast_fusion.33), kind=kCustom, calls=%fused_computation.26 | custom fusion | flops 16384 | bytes 262144
  384.5 16.9 %all-gather.8.cloned.1.call-done = f32[512,512]{1,0:T(8,128)} async-done(((f32[128,512]{1,0:T(8,128)}), f32[512,512]{1,0:T(8,128)}) %all-gather.8.cloned.1.call-update) | async-done | bytes 1048592 | tf_op jit(solution)/shard_map/all_gather | solution.py:43
  403.1 23.8 %collective-permute-done.2 = f32[512,512]{1,0:T(8,128)S(1)} collective-permute-done((f32[512,512]{1,0:T(8,128)}, f32[512,512]{1,0:T(8,128)S(1)}, u32[]{:S(2)}, u32[]{:S(2)}) %collective-permute-start.2) | collective-permute-done | bytes 1048608 | tf_op jit(solution)/shard_map/ppermute | solution.py:20
  438.8 11.7 cholesky.534
  463.7 11.7 cholesky.553
  487.7 11.7 cholesky.574
  511.3 11.9 cholesky.591
  527.9 11.9 while.9
  539.8 39.3 %custom-call.58 = f32[4,128,128]{1,2,0:T(8,128)S(1)} custom-call(f32[4,128,128]{2,1,0:T(8,128)S(1)} %get-tuple-element.106), custom_call_target="InvertDiagBlocksLowerTriangular" | custom-call | tf_op jit(solution)/shard_map/jit(_solve_triangular)/triangular_solve | solution.py:97
  629.8 19.2 %collective-permute-done.5 = f32[512,512]{1,0:T(8,128)S(1)} collective-permute-done((f32[512,512]{1,0:T(8,128)}, f32[512,512]{1,0:T(8,128)S(1)}, u32[]{:S(2)}, u32[]{:S(2)}) %collective-permute-start.5) | collective-permute-done | bytes 1048608 | tf_op jit(solution)/shard_map/ppermute | solution.py:20
  663.0 57.0 %scatter_fusion.4 = f32[65536]{0:T(1024)S(1)} fusion(f32[65536]{0:T(1024)S(1)} %bitcast.323, s32[8192]{0:T(1024)S(1)} %copy-done.22, f32[8192]{0:T(1024)S(1)} %copy-done.21), kind=kCustom, calls=%fused_computation.27 | custom fusion | flops 8192 | bytes 131072
  728.5 12.7 collective-permute-done.6
  742.9 23.2 %collective-permute-done.7 = f32[512,512]{1,0:T(8,128)} collective-permute-done((f32[512,512]{1,0:T(8,128)S(1)}, f32[512,512]{1,0:T(8,128)}, u32[]{:S(2)}, u32[]{:S(2)}) %collective-permute-start.7) | collective-permute-done | bytes 1048608 | tf_op jit(solution)/shard_map/ppermute | solution.py:20
  777.6 11.7 cholesky.606
  850.2 12.1 cholesky.663
  878.8 39.3 %custom-call.62 = f32[4,128,128]{1,2,0:T(8,128)S(1)} custom-call(f32[4,128,128]{2,1,0:T(8,128)S(1)} %get-tuple-element.107), custom_call_target="InvertDiagBlocksLowerTriangular" | custom-call | tf_op jit(solution)/shard_map/jit(_solve_triangular)/triangular_solve | solution.py:97
  972.1 42.3 %collective-permute-done.11 = f32[512,512]{1,0:T(8,128)S(1)} collective-permute-done((f32[512,512]{1,0:T(8,128)}, f32[512,512]{1,0:T(8,128)S(1)}, u32[]{:S(2)}, u32[]{:S(2)}) %collective-permute-start.11) | collective-permute-done | bytes 1048608 | tf_op jit(solution)/shard_map/ppermute | solution.py:20
  1028.5 28.8 %scatter_fusion.5 = f32[32768]{0:T(1024)S(1)} fusion(f32[32768]{0:T(1024)S(1)} %bitcast.324, s32[4096]{0:T(1024)S(1)} %copy-done.26, f32[4096]{0:T(1024)S(1)} %copy-done.25), kind=kCustom, calls=%fused_computation.28 | custom fusion | flops 4096 | bytes 65536
  1071.9 13.4 collective-permute-done.13
  1105.2 28.6 %collective-permute-done.14 = f32[512,512]{1,0:T(8,128)} collective-permute-done((f32[512,512]{1,0:T(8,128)}, f32[512,512]{1,0:T(8,128)}, u32[]{:S(2)}, u32[]{:S(2)}) %collective-permute-start.14) | collective-permute-done | bytes 1048608 | tf_op jit(solution)/shard_map/ppermute | solution.py:20
  1217.2 11.9 cholesky.735
  1245.3 39.3 %custom-call.66 = f32[4,128,128]{1,2,0:T(8,128)S(1)} custom-call(f32[4,128,128]{2,1,0:T(8,128)S(1)} %get-tuple-element.108), custom_call_target="InvertDiagBlocksLowerTriangular" | custom-call | tf_op jit(solution)/shard_map/jit(_solve_triangular)/triangular_solve | solution.py:97
  1300.2 37.2 %psum.7 = f32[]{:T(128)} all-reduce(f32[]{:T(128)S(6)} %add.415), channel_id=1, replica_groups=mesh['leaf'=8,'front'=4] {'leaf','front'}, use_global_device_ids=true, to_apply=%region_39.48 | all-reduce | flops 1 | bytes 8 | tf_op jit(solution)/shard_map/psum | solution.py:156
  (528 shorter events, 578.0 us)
Async XLA Ops:
  7.2 28.7 %all-gather.4.cloned.1.call-start = ((), (), s32[]{:S(2)}) async-start(), calls=%async_computation | async-start | bytes 2621440 | tf_op jit(solution)/shard_map/all_gather | solution.py:43
  10.4 217.6 %all-gather.6.cloned.1.call-start = ((), (), s32[]{:S(2)}) async-start(), calls=%async_computation.1 | async-start | bytes 1310720 | tf_op jit(solution)/shard_map/all_gather | solution.py:45
  130.2 52.7 %copy-start.7 = (f32[512,512]{0,1:T(8,128)S(1)}, f32[512,512]{0,1:T(8,128)}, u32[]{:S(2)}) copy-start(f32[512,512]{0,1:T(8,128)} %get-tuple-element.245) | copy-start | bytes 3145732
  196.8 34.0 %copy-start.24 = (f32[1,1,224,128]{3,2,1,0:T(8,128)S(1)}, f32[1,1,224,128]{3,2,1,0:T(8,128)}, u32[]{:S(2)}) copy-start(f32[1,1,224,128]{3,2,1,0:T(8,128)} %param.28) | copy-start | bytes 344068
  198.7 10.5 collective-permute-start
  210.9 190.5 %all-gather.8.cloned.1.call-start = ((), (), s32[]{:S(2)}) async-start(), calls=%async_computation.2 | async-start | bytes 1310720 | tf_op jit(solution)/shard_map/all_gather | solution.py:43
  212.7 42.3 %copy-start.37 = (s32[128]{0:T(128)}, s32[128]{0:T(128)S(1)}, u32[]{:S(2)}) copy-start(s32[128]{0:T(128)S(1)} %get-tuple-element.165) | copy-start | bytes 1540
  212.7 42.3 %copy-start.39 = (s32[128]{0:T(128)}, s32[128]{0:T(128)S(1)}, u32[]{:S(2)}) copy-start(s32[128]{0:T(128)S(1)} %get-tuple-element.164) | copy-start | bytes 1540
  228.0 25.5 %collective-permute-start.1 = (f32[512,512]{1,0:T(8,128)}, f32[512,512]{1,0:T(8,128)S(1)}, u32[]{:S(2)}, u32[]{:S(2)}) collective-permute-start(f32[512,512]{1,0:T(8,128)} %all-gather.6.cloned.1.call-done), channel_id=1, source_target_pairs={{0,4},{4,0},{8,12},{12,8},{16,20},{20,16},{24,28},{28,24},{1,5},{5... | collective-permute-start | bytes 3145736 | tf_op jit(solution)/shard_map/ppermute | solution.py:20
  270.1 132.8 %copy-start.27 = (s32[1,512]{1,0:T(1,128)S(1)}, s32[1,512]{1,0:T(1,128)}, u32[]{:S(2)}) copy-start(s32[1,512]{1,0:T(1,128)} %get-tuple-element.305) | copy-start | bytes 6148
  270.1 132.8 %copy-start.29 = (s32[1,512]{1,0:T(1,128)S(1)}, s32[1,512]{1,0:T(1,128)}, u32[]{:S(2)}) copy-start(s32[1,512]{1,0:T(1,128)} %get-tuple-element.307) | copy-start | bytes 6148
  401.4 25.5 %collective-permute-start.2 = (f32[512,512]{1,0:T(8,128)}, f32[512,512]{1,0:T(8,128)S(1)}, u32[]{:S(2)}, u32[]{:S(2)}) collective-permute-start(f32[512,512]{1,0:T(8,128)} %all-gather.8.cloned.1.call-done), channel_id=1, source_target_pairs={{0,4},{4,0},{8,12},{12,8},{16,20},{20,16},{24,28},{28,24},{1,5},{5... | collective-permute-start | bytes 3145736 | tf_op jit(solution)/shard_map/ppermute | solution.py:20
  402.9 223.1 %copy-start.41 = (s32[64]{0:T(128)}, s32[64]{0:T(128)S(1)}, u32[]{:S(2)}) copy-start(s32[64]{0:T(128)S(1)} %iota_add_fusion.2) | copy-start | bytes 772
  403.1 224.1 %copy-start.33 = (s32[64]{0:T(128)}, s32[64]{0:T(128)S(1)}, u32[]{:S(2)}) copy-start(s32[64]{0:T(128)S(1)} %get-tuple-element.161) | copy-start | bytes 772
  526.3 52.8 %copy-start.4 = (f32[512,512]{0,1:T(8,128)S(1)}, f32[512,512]{0,1:T(8,128)}, u32[]{:S(2)}) copy-start(f32[512,512]{0,1:T(8,128)} %get-tuple-element.239) | copy-start | bytes 3145732
  592.5 8.5 collective-permute-start.3
  607.6 15.2 %collective-permute-start.4 = (f32[256,512]{1,0:T(8,128)S(1)}, f32[256,512]{1,0:T(8,128)S(1)}, u32[]{:S(2)}, u32[]{:S(2)}) collective-permute-start(f32[256,512]{1,0:T(8,128)S(1)} %all_gather.24), channel_id=1, source_target_pairs={{0,4},{4,0},{8,12},{12,8},{16,20},{20,16},{24,28},{28,24},{1,5},{5... | collective-permute-start | bytes 1572872 | tf_op jit(solution)/shard_map/ppermute | solution.py:20
  623.9 25.0 %collective-permute-start.5 = (f32[512,512]{1,0:T(8,128)}, f32[512,512]{1,0:T(8,128)S(1)}, u32[]{:S(2)}, u32[]{:S(2)}) collective-permute-start(f32[512,512]{1,0:T(8,128)} %pad_maximum_fusion.5), channel_id=1, source_target_pairs={{0,8},{8,0},{4,12},{12,4},{16,24},{24,16},{20,28},{28,20},{1,9},{9... | collective-permute-start | bytes 3145736 | tf_op jit(solution)/shard_map/ppermute | solution.py:20
  727.0 14.2 %collective-permute-start.6 = (f32[256,512]{1,0:T(8,128)S(1)}, f32[256,512]{1,0:T(8,128)S(1)}, u32[]{:S(2)}, u32[]{:S(2)}) collective-permute-start(f32[256,512]{1,0:T(8,128)S(1)} %all_gather.25), channel_id=1, source_target_pairs={{0,4},{4,0},{8,12},{12,8},{16,20},{20,16},{24,28},{28,24},{1,5},{5... | collective-permute-start | bytes 1572872 | tf_op jit(solution)/shard_map/ppermute | solution.py:20
  741.3 24.8 %collective-permute-start.7 = (f32[512,512]{1,0:T(8,128)S(1)}, f32[512,512]{1,0:T(8,128)}, u32[]{:S(2)}, u32[]{:S(2)}) collective-permute-start(f32[512,512]{1,0:T(8,128)S(1)} %pad_maximum_fusion.6), channel_id=1, source_target_pairs={{0,8},{8,0},{4,12},{12,4},{16,24},{24,16},{20,28},{28,20},{1,9},{9... | collective-permute-start | bytes 3145736 | tf_op jit(solution)/shard_map/ppermute | solution.py:20
  865.4 52.7 %copy-start.3 = (f32[512,512]{0,1:T(8,128)S(1)}, f32[512,512]{0,1:T(8,128)}, u32[]{:S(2)}) copy-start(f32[512,512]{0,1:T(8,128)} %get-tuple-element.233) | copy-start | bytes 3145732
  929.7 25.0 %copy-start.49 = (s32[2]{0:T(128)S(1)}, s32[2]{0:T(128)}, u32[]{:S(2)}) copy-start(s32[2]{0:T(128)} %constant.355) | copy-start | bytes 28
  929.7 25.0 %copy-start.59 = (s32[2]{0:T(128)S(1)}, s32[2]{0:T(128)}, u32[]{:S(2)}) copy-start(s32[2]{0:T(128)} %constant.370) | copy-start | bytes 28
  929.7 7.7 collective-permute-start.8
  931.0 37.1 %copy-start.43 = (s32[32]{0:T(128)}, s32[32]{0:T(128)S(1)}, u32[]{:S(2)}) copy-start(s32[32]{0:T(128)S(1)} %iota_add_fusion.1) | copy-start | bytes 388
  943.2 8.6 collective-permute-start.9
  944.9 24.7 %copy-start.35 = (s32[32]{0:T(128)}, s32[32]{0:T(128)S(1)}, u32[]{:S(2)}) copy-start(s32[32]{0:T(128)S(1)} %get-tuple-element.157) | copy-start | bytes 388
  951.8 13.7 %collective-permute-start.10 = (f32[256,512]{1,0:T(8,128)S(1)}, f32[256,512]{1,0:T(8,128)S(1)}, u32[]{:S(2)}, u32[]{:S(2)}) collective-permute-start(f32[256,512]{1,0:T(8,128)S(1)} %pad_maximum_fusion.10), channel_id=1, source_target_pairs={{0,8},{8,0},{4,12},{12,4},{16,24},{24,16},{20,28},{28,20},{1,9},{9... | collective-permute-start | bytes 1572872 | tf_op jit(solution)/shard_map/ppermute | solution.py:20
  966.7 47.6 %collective-permute-start.11 = (f32[512,512]{1,0:T(8,128)}, f32[512,512]{1,0:T(8,128)S(1)}, u32[]{:S(2)}, u32[]{:S(2)}) collective-permute-start(f32[512,512]{1,0:T(8,128)} %pad_maximum_fusion.8), channel_id=1, source_target_pairs={{0,16},{16,0},{4,20},{20,4},{8,24},{24,8},{12,28},{28,12},{1,17},{... | collective-permute-start | bytes 3145736 | tf_op jit(solution)/shard_map/ppermute | solution.py:20
  1063.1 8.6 collective-permute-start.12
  1071.8 13.4 collective-permute-start.13
  1086.4 47.4 %collective-permute-start.14 = (f32[512,512]{1,0:T(8,128)}, f32[512,512]{1,0:T(8,128)}, u32[]{:S(2)}, u32[]{:S(2)}) collective-permute-start(f32[512,512]{1,0:T(8,128)} %pad_maximum_fusion.9), channel_id=1, source_target_pairs={{0,16},{16,0},{4,20},{20,4},{8,24},{24,8},{12,28},{28,12},{1,17},{... | collective-permute-start | bytes 3145736 | tf_op jit(solution)/shard_map/ppermute | solution.py:20
  (51 other events, 335.8 us)
Sparse Core Ops, SparseCore 0:
  10.6 25.2 all-gather.3
  211.0 16.9 all-gather.5
  384.7 16.7 all-gather.7
where the time goes:
time: 1360 us; the launch traced here: 1350 us
  other arithmetic  746 us (55%)
  waiting for transfers between devices  300 us (22%)
  local copies, waits for them, and re-layouts  133 us (10%)
  blocking collectives  62.2 us (5%)
  matrix products  56.4 us (4%)
  between operations  30.8 us (2%)
  starting transfers between devices  20.3 us (1%)
    another operation x59, other arithmetic, body(): chol_head = jnp.linalg.cholesky(head_block)  318 us
    ppermute x12, waiting for transfers between devices, swapped(): return lax.ppermute(block, axis, route)  222 us
    unnamed x12, other arithmetic  201 us
    another operation x12, other arithmetic, body(): jax.scipy.linalg.solve_triangular(chol_head, panel_cols[SEP:].T, lower=True)  168 us
    all_gather x3, waiting for transfers between devices, collect(): gathered = lax.all_gather(strip_piece, 'front', axis=0, tiled=True)  55.6 us
    another operation x65, local copies, waits for them, and re-layouts, body(): jax.scipy.linalg.solve_triangular(chol_head, panel_cols[SEP:].T, lower=True)  52.9 us
    another operation x28, matrix products, body(): jax.scipy.linalg.solve_triangular(chol_head, panel_cols[SEP:].T, lower=True)  38.2 us
    psum x1, blocking collectives, body(): log_det = 2.0 * lax.psum(log_part, ('leaf', 'front'))  37.2 us
  transfers between devices with their start and end apart: 18, of which 18 were waited for; matrix products, arithmetic and copies ran while one was open for 2% of the time, Pallas kernels for 0%

commit v1 on v0

v1 whole, which is shorter than its diff:
```python
import functools

import jax
import jax.numpy as jnp
from jax import lax
from jax.experimental import pallas as pl
from jax.experimental.pallas import tpu as pltpu
from jax.sharding import Mesh, PartitionSpec as P

SEP = 512
BND = 512
WIDTH = SEP + BND
KC = 128
T = 128
NB = SEP // T
TILE = 256
NPACK = NB * (NB + 1) // 2
F32 = jnp.float32
BF16 = jnp.bfloat16
VMEM_LIMIT = 50 * 1024 * 1024


def pack_index(i, j):
    return i * (i + 1) // 2 + j


def split(x):
    hi = x.astype(BF16)
    return hi, (x - hi.astype(F32)).astype(BF16)


def dot_nt(a, b):
    return lax.dot_general(a, b, (((1,), (1,)), ((), ())), preferred_element_type=F32)


def dot_nn(a, b):
    return lax.dot_general(a, b, (((1,), (0,)), ((), ())), preferred_element_type=F32)


def mm_nt(a, b):
    a_hi, a_lo = split(a)
    b_hi, b_lo = split(b)
    return dot_nt(a_hi, b_hi) + (dot_nt(a_hi, b_lo) + dot_nt(a_lo, b_hi))


def iota2(shape, dim):
    return lax.broadcasted_iota(jnp.int32, shape, dim)


def tri_sym(block):
    n = block.shape[0]
    rows, cols = iota2((n, n), 0), iota2((n, n), 1)
    low = jnp.where(cols <= rows, block, 0.0)
    strict = jnp.where(cols < rows, block, 0.0)
    return low + strict.T


def chol_and_inverse(sym):
    lane, sub = iota2((8, T), 1), iota2((8, T), 0)
    groups = [sym[8 * g : 8 * g + 8] for g in range(T // 8)]
    upper_rows, inv_rows = [], []
    for s in range(T // 8):
        c = 8 * s
        panel = groups[s]
        inside = (lane >= c) & (lane < c + 8)
        cols = [jnp.broadcast_to(panel[:, c + k : c + k + 1], (8, T)) for k in range(8)]
        plain = panel
        aug = jnp.where(inside, jnp.where(lane - c == sub, 1.0, 0.0), panel)
        upper_acc = jnp.zeros((8, T), F32)
        inv_acc = jnp.zeros((8, T), F32)
        for k in range(8):
            at_k = sub == k
            pivot = jnp.broadcast_to(cols[k][k : k + 1], (8, T))
            recip = 1.0 / pivot
            root = lax.rsqrt(pivot)
            plain_row = jnp.broadcast_to(plain[k : k + 1], (8, T))
            aug_row = jnp.broadcast_to(aug[k : k + 1], (8, T))
            upper_acc = jnp.where(at_k, plain_row * root, upper_acc)
            inv_acc = jnp.where(at_k, aug_row * root, inv_acc)
            plain = plain - cols[k] * (plain_row * recip)
            scaled = aug_row * recip
            aug = jnp.where(at_k, scaled, aug - cols[k] * scaled)
            for m in range(k + 1, 8):
                term = jnp.broadcast_to(cols[m][k : k + 1], (8, T)) * recip
                cols[m] = jnp.where(at_k, term, cols[m] - cols[k] * term)
        upper_rows.append(jnp.where(lane >= c + sub, upper_acc, 0.0))
        inv_rows.append(jnp.where(lane <= c + sub, inv_acc, 0.0))
        sol = [jnp.broadcast_to(aug[k : k + 1], (8, T)) for k in range(8)]
        for g in range(s + 1, T // 8):
            old = groups[g]
            terms = [
                jnp.broadcast_to(old[:, c + k : c + k + 1], (8, T)) * sol[k] for k in range(8)
            ]
            total = ((terms[0] + terms[1]) + (terms[2] + terms[3])) + (
                (terms[4] + terms[5]) + (terms[6] + terms[7])
            )
            groups[g] = jnp.where(inside, 0.0, old) - total
    return jnp.concatenate(upper_rows, axis=0), jnp.concatenate(inv_rows, axis=0)


def factor_panel(f_ref, x_ref, log_ref, rows):
    log_ref[...] = jnp.zeros_like(log_ref)

    @pl.loop(0, NB)
    def _(j):
        at = pl.multiple_of(j * T, T)
        upper, inv = chol_and_inverse(tri_sym(f_ref[pl.ds(at, T), pl.ds(at, T)]))
        f_ref[pl.ds(at, T), pl.ds(at, T)] = upper.T
        x_ref[pl.ds(at, T), :] = inv
        eye = iota2((T, T), 0) == iota2((T, T), 1)
        diag = jnp.sum(jnp.where(eye, upper, 0.0), axis=0, keepdims=True)
        log_ref[0:1, :] += jnp.log(diag)
        for k in range(NB):
            first = (k + 1) * T
            if first >= rows:
                continue

            @pl.when(j == k)
            def _():
                below = mm_nt(f_ref[first:rows, k * T : first], inv)
                f_ref[first:rows, k * T : first] = below
                if first < SEP:
                    f_ref[first:rows, first:SEP] -= mm_nt(below, below[: SEP - first])


def zero_above(f_ref):
    for i in range(NB - 1):
        f_ref[i * T : (i + 1) * T, (i + 1) * T : SEP] = jnp.zeros((T, SEP - (i + 1) * T), F32)


def log_total(log_ref):
    return 2.0 * jnp.sum(log_ref[0:1, :], axis=1, keepdims=True)


def write_own(out_ref, f_ref, start):
    size = out_ref.shape[0]
    if size % 8 == 0:
        out_ref[...] = f_ref[pl.ds(pl.multiple_of(start, 8), size), 0:SEP]
    else:
        base = pl.multiple_of(start // 8 * 8, 8)
        block = f_ref[pl.ds(base, 8), 0:SEP]
        offset = start - base
        piece = block[0:size]
        for shift in range(size, 8, size):
            piece = jnp.where(offset == shift, block[shift : shift + size], piece)
        out_ref[...] = piece


def write_update(pk_ref, below, tail_of, log_value):
    hi, lo = split(below)
    rows, cols = iota2((T, T), 0), iota2((T, T), 1)
    for i in range(NB):
        here = slice(i * T, (i + 1) * T)
        upto = slice(0, (i + 1) * T)
        prod = dot_nt(hi[here], hi[upto]) + (dot_nt(hi[here], lo[upto]) + dot_nt(lo[here], hi[upto]))
        for j in range(i + 1):
            block = tail_of(i, j) - prod[:, j * T : (j + 1) * T]
            if i == 0:
                block = jnp.where((rows == 0) & (cols == T - 1), log_value, block)
            pk_ref[pack_index(i, j)] = block


def head_kernel(head_ref, fac_ref, x_ref, log_ref):
    fac_ref[...] = head_ref[...]
    factor_panel(fac_ref, x_ref, log_ref, SEP)
    zero_above(fac_ref)


def leaf_kernel(pos_ref, fac_ref, x_ref, log_ref, panel_ref, tail_ref, own_ref, pk_ref, work, stack):
    work[...] = panel_ref[...]
    for j in range(NB):
        here = slice(j * T, (j + 1) * T)
        solved = mm_nt(work[:, here], x_ref[here, :])
        work[:, here] = solved
        if j + 1 < NB:
            rest = slice((j + 1) * T, SEP)
            work[:, rest] -= mm_nt(solved, fac_ref[rest, here])
    stack[0:SEP, :] = fac_ref[...]
    stack[SEP:, :] = work[...]
    write_own(own_ref, stack, pos_ref[1] * own_ref.shape[0])

    def tail_of(i, j):
        return tail_ref[i * T : (i + 1) * T, j * T : (j + 1) * T]

    write_update(pk_ref, work[...], tail_of, log_total(log_ref))


def assemble(level, n_leaf, pos_ref, kids, maps_ref, dense_ref, diag_ref, f_ref, u_hi, u_lo, hot, y_hi, y_lo, last):
    leaf = pos_ref[0]
    base = 2 * n_leaf - 2 * (n_leaf >> (level - 1))
    own = leaf >> (level - 1)
    rows, cols = iota2((T, T), 0), iota2((T, T), 1)
    for child, pk_ref in enumerate(kids):
        number = base + (own if child == 0 else own ^ 1)
        for i in range(NB):
            for j in range(i + 1):
                block = pk_ref[pack_index(i, j)]
                if i == j:
                    low = jnp.where(cols <= rows, block, 0.0)
                    block = low + jnp.where(cols < rows, block, 0.0).T
                hi, lo = split(block)
                u_hi[i * T : (i + 1) * T, j * T : (j + 1) * T] = hi
                u_lo[i * T : (i + 1) * T, j * T : (j + 1) * T] = lo
                if i != j:
                    hi, lo = split(block.T)
                    u_hi[j * T : (j + 1) * T, i * T : (i + 1) * T] = hi
                    u_lo[j * T : (j + 1) * T, i * T : (i + 1) * T] = lo
        index_row = maps_ref[pl.ds(number, 1), :]

        @pl.loop(0, WIDTH // TILE)
        def _(tile):
            at = pl.multiple_of(tile * TILE, TILE)
            ids = iota2((TILE, BND), 0) + at
            match = jnp.where(ids == index_row, 1.0, 0.0).astype(BF16)
            hot[child, pl.ds(at, TILE), :] = match
            y_hi[child, pl.ds(at, TILE), :] = dot_nn(match, u_hi[...]).astype(BF16)
            y_lo[child, pl.ds(at, TILE), :] = dot_nn(match, u_lo[...]).astype(BF16)

    for a in range(WIDTH // TILE):
        here = slice(a * TILE, (a + 1) * TILE)
        for b in range(a + 1):
            if last and b * TILE >= SEP:
                continue
            there = slice(b * TILE, (b + 1) * TILE)
            parts = [
                dot_nt(y_hi[c, here, :], hot[c, there, :]) + dot_nt(y_lo[c, here, :], hot[c, there, :])
                for c in range(2)
            ]
            total = parts[0] + parts[1]
            for h in range(TILE // T):
                col_block = b * (TILE // T) + h
                piece = total[:, h * T : (h + 1) * T] + dense_ref[col_block, here, :]
                f_ref[here, col_block * T : (col_block + 1) * T] = piece
    for d in range((SEP if last else WIDTH) // T):
        spot = slice(d * T, (d + 1) * T)
        f_ref[spot, spot] += jnp.where(rows == cols, diag_ref[d : d + 1, :], 0.0)


def level_kernel(
    level, n_leaf, n_front, last,
    pos_ref, own_pk, sib_pk, maps_ref, dense_ref, diag_ref,
    own_ref, next_ref,
    f_ref, x_ref, log_ref, u_hi, u_lo, hot, y_hi, y_lo,
):
    assemble(
        level, n_leaf, pos_ref, (own_pk, sib_pk), maps_ref, dense_ref, diag_ref,
        f_ref, u_hi, u_lo, hot, y_hi, y_lo, last,
    )
    factor_panel(f_ref, x_ref, log_ref, WIDTH)
    zero_above(f_ref)
    rank = (pos_ref[0] & ((1 << level) - 1)) * n_front + pos_ref[1]
    write_own(own_ref, f_ref, rank * own_ref.shape[0])
    kids_log = own_pk[0][0:1, T - 1 : T] + sib_pk[0][0:1, T - 1 : T]
    log_value = kids_log + log_total(log_ref)
    if last:
        next_ref[...] = jnp.broadcast_to(log_value, next_ref.shape)
    else:

        def tail_of(i, j):
            return f_ref[SEP + i * T : SEP + (i + 1) * T, SEP + j * T : SEP + (j + 1) * T]

        write_update(next_ref, f_ref[SEP:, 0:SEP], tail_of, log_value)


def densify_kernel(lists_ref, out_ref):
    block_ids = iota2((8, KC), 0).astype(F32)
    column_ids = iota2((T, KC), 0).astype(F32)

    @pl.loop(0, WIDTH // 8)
    def _(group):
        at = pl.multiple_of(group * 8, 8)
        cols = lists_ref[pl.ds(at, 8), 0:KC]
        vals = lists_ref[pl.ds(at, 8), KC:]
        block_no = jnp.floor(cols * (1.0 / T))
        within = cols - block_no * T
        hi = vals.astype(BF16).astype(F32)
        lo = vals - hi
        for r in range(8):
            pick = block_ids == block_no[r : r + 1]
            left = jnp.concatenate(
                [jnp.where(pick, hi[r : r + 1], 0.0), jnp.where(pick, lo[r : r + 1], 0.0)], axis=0
            ).astype(BF16)
            right = jnp.where(column_ids == within[r : r + 1], 1.0, 0.0).astype(BF16)
            both = dot_nt(left, right)
            out_ref[pl.ds(at + r, 8, stride=WIDTH), :] = both[0:8] + both[8:16]


def params():
    return pltpu.CompilerParams(vmem_limit_bytes=VMEM_LIMIT)


def vmem():
    return pl.BlockSpec(memory_space=pltpu.VMEM)


def smem():
    return pl.BlockSpec(memory_space=pltpu.SMEM)


def shape(*dims):
    return jax.ShapeDtypeStruct(dims, F32)


def cost(us):
    return pl.CostEstimate(flops=0, bytes_accessed=int(us * 3.0e6), transcendentals=0)


def densify(lists):
    out = pl.pallas_call(
        densify_kernel,
        out_shape=shape(WIDTH // T * WIDTH, T),
        in_specs=[vmem()],
        out_specs=vmem(),
        compiler_params=params(),
        cost_estimate=cost(12),
        name="densify",
    )(lists)
    return out.reshape(WIDTH // T, WIDTH, T)


def run_head(head):
    return pl.pallas_call(
        head_kernel,
        out_shape=(shape(SEP, SEP), shape(SEP, T), shape(8, T)),
        in_specs=[vmem()],
        out_specs=(vmem(),) * 3,
        compiler_params=params(),
        cost_estimate=cost(25),
        name="head_factor",
    )(head)


def run_leaf(pos, fac, inv, logs, panel, tail, size_rows):
    return pl.pallas_call(
        leaf_kernel,
        out_shape=(shape(size_rows, SEP), shape(NPACK, T, T)),
        in_specs=[smem()] + [vmem()] * 5,
        out_specs=(vmem(),) * 2,
        scratch_shapes=[pltpu.VMEM((BND, SEP), F32), pltpu.VMEM((WIDTH, SEP), F32)],
        compiler_params=params(),
        cost_estimate=cost(5),
        name="leaf_update",
    )(pos, fac, inv, logs, panel, tail)


def run_level(level, n_leaf, n_front, last, pos, own_pk, sib_pk, maps, dense, diag, size_rows):
    return pl.pallas_call(
        functools.partial(level_kernel, level, n_leaf, n_front, last),
        out_shape=(shape(size_rows, SEP), shape(8, T) if last else shape(NPACK, T, T)),
        in_specs=[smem()] + [vmem()] * 5,
        out_specs=(vmem(),) * 2,
        scratch_shapes=[
            pltpu.VMEM((WIDTH, WIDTH), F32),
            pltpu.VMEM((SEP, T), F32),
            pltpu.VMEM((8, T), F32),
            pltpu.VMEM((BND, BND), BF16),
            pltpu.VMEM((BND, BND), BF16),
            pltpu.VMEM((2, WIDTH, BND), BF16),
            pltpu.VMEM((2, WIDTH, BND), BF16),
            pltpu.VMEM((2, WIDTH, BND), BF16),
        ],
        compiler_params=params(),
        cost_estimate=cost(35),
        name="level_front",
    )(pos, own_pk, sib_pk, maps, dense, diag)


def swap_front(x, mask):
    count = lax.axis_size("front")
    return lax.ppermute(x, "front", [(f, f ^ mask) for f in range(count)])


def double_up(x, bits, front):
    for b in range(bits):
        partner = swap_front(x, 1 << b)
        high = (front >> b & 1) == 1
        x = jnp.concatenate([jnp.where(high, partner, x), jnp.where(high, x, partner)], axis=0)
    return x


def body(leaf_bits, leaf_fronts, coupling_cols, coupling_vals, sep_diag, child_maps):
    n_front = lax.axis_size("front")
    bits = len(leaf_bits)
    n_leaf = 1 << bits
    front = lax.axis_index("front")
    leaf = lax.axis_index(leaf_bits) if bits else 0
    pos = jnp.stack([leaf, front]).astype(jnp.int32)
    strip = leaf_fronts[0]
    half = n_front // 2
    half_bits = half.bit_length() - 1
    in_tail = front >= half

    panel_strip = strip[:, :SEP]
    other_strip = swap_front(panel_strip, half)
    own_half = double_up(panel_strip, half_bits, front)
    other_half = double_up(other_strip, half_bits, front)
    head = jnp.where(in_tail, other_half, own_half)
    panel = jnp.where(in_tail, own_half, other_half)
    tail_strip = strip[:, SEP:]
    sent = lax.ppermute(tail_strip, "front", [(f, f - half) for f in range(half, n_front)])
    tail = double_up(jnp.where(in_tail, tail_strip, sent), half_bits, front)

    lists, diags = [], []
    offset = 0
    for level in range(1, bits + 1):
        size_rows = WIDTH // (n_front << level)
        span = slice(offset, offset + size_rows)
        entries = jnp.concatenate(
            [coupling_cols[0, 0, span].astype(F32), coupling_vals[0, 0, span]], axis=1
        )
        diag_row = jnp.pad(sep_diag[0, 0, span], (0, 2 * KC - size_rows))[None]
        packed = jnp.concatenate([entries, jnp.pad(diag_row, ((0, 7), (0, 0)))], axis=0)
        axes = leaf_bits[bits - level :] + ("front",)
        gathered = lax.all_gather(packed, axes, axis=0, tiled=False)
        lists.append(gathered[:, :size_rows].reshape(WIDTH, 2 * KC))
        diags.append(gathered[:, size_rows, :size_rows].reshape(WIDTH // T, T))
        offset += size_rows

    fac, inv, logs = run_head(head)
    piece, pk = run_leaf(pos, fac, inv, logs, panel, tail, WIDTH // n_front)
    pieces = [piece]
    for level in range(1, bits + 1):
        size_rows = WIDTH // (n_front << level)
        last = level == bits
        sib = lax.ppermute(pk, leaf_bits[bits - level], [(0, 1), (1, 0)])
        dense = densify(lists[level - 1])
        piece, pk = run_level(
            level, n_leaf, n_front, last, pos, pk, sib, child_maps, dense, diags[level - 1], size_rows
        )
        pieces.append(piece)
    log_det = pk[0, 0]
    return jnp.concatenate(pieces, axis=0)[None, None], log_det


def solution(mesh):
    bits = mesh.shape["leaf"].bit_length() - 1
    leaf_bits = tuple(f"leaf{b}" for b in reversed(range(bits)))
    fine = Mesh(mesh.devices.reshape((2,) * bits + (mesh.shape["front"],)), leaf_bits + ("front",))
    placed = (
        P(leaf_bits, "front", None),
        P(leaf_bits, "front", None, None),
        P(leaf_bits, "front", None, None),
        P(leaf_bits, "front", None),
        P(),
    )
    return jax.shard_map(
        functools.partial(body, leaf_bits),
        mesh=fine,
        in_specs=placed,
        out_specs=(P(leaf_bits, "front", None, None), P()),
        check_vma=False,
    )
```

time: 1360 us -> 298 us (0.22)
  other arithmetic: 746 us -> 8.26 us
  waiting for transfers between devices: 300 us -> 24.2 us
  Pallas kernels: 0 us -> 227 us
  local copies, waits for them, and re-layouts: 133 us -> 12.8 us
  blocking collectives: 62.2 us -> 0 us
  matrix products: 56.4 us -> 0 us
  between operations: 30.8 us -> 13.9 us
    another operation x74 -> x1, other arithmetic: 487 us -> 0.08 us  [body(): pos = jnp.stack([leaf, front]).astype(jnp.int32)]
    pallas_call x0 -> x8, Pallas kernels: none -> 227 us  [the longest x3 107 us: densify(): pl.pallas_call(densify_kernel, out_shape=shape(WIDTH // T * WIDTH, T), in...]
    ppermute x15 -> x8, waiting for transfers between devices: 245 us -> 24.1 us  [the longest x1 13.3 us: body(): lax.ppermute(tail_strip, 'front', [(f, f - half) for f in range(half, n_f...]
    unnamed x12 -> x0, other arithmetic: 201 us -> none
    another operation x52 -> x0, matrix products: 56.4 us -> none  [the longest x28 38.2 us: body(): jax.scipy.linalg.solve_triangular(chol_head, panel_cols[SEP:].T, lower=True)]
    all_gather x3, waiting for transfers between devices: 55.6 us -> 0.01 us  [body(): gathered = lax.all_gather(packed, axes, axis=0, tiled=False)]
    another operation x87 -> x2, local copies, waits for them, and re-layouts: 54.8 us -> 0.14 us  [body(): diags.append(gathered[:, size_rows, :size_rows].reshape(WIDTH // T, T))]
    gather x20 -> x0, local copies, waits for them, and re-layouts: 46.8 us -> none  [the longest x4 18.9 us: symmetric_of(): return lower_tri + lower_tri.T - jnp.diag(jnp.diag(lower_tri))]
  transfers between devices with their start and end apart: 18 -> 11, of which waited for: 18 -> 2; matrix products, arithmetic and copies ran while one was open for 2% -> 6% of each run, Pallas kernels for 0% -> 66%
where the time goes in v1:
time: 298 us; the launch traced here: 297 us
  Pallas kernels  227 us (76%)
  waiting for transfers between devices  24.2 us (8%)
  between operations  13.9 us (5%)
  local copies, waits for them, and re-layouts  12.8 us (4%)
  starting transfers between devices  10.7 us (4%)
  other arithmetic  8.26 us (3%)
    pallas_call x3, Pallas kernels, densify(): pl.pallas_call(densify_kernel, out_shape=shape(WIDTH // T * WIDTH, T), in...  107 us
    pallas_call x3, Pallas kernels, run_level(): pl.pallas_call(functools.partial(level_kernel, level, n_leaf, n_front, la...  95.8 us
    pallas_call x1, Pallas kernels, run_head(): pl.pallas_call(head_kernel, out_shape=(shape(SEP, SEP), shape(SEP, T), sh...  20.3 us
    ppermute x1, waiting for transfers between devices, body(): lax.ppermute(tail_strip, 'front', [(f, f - half) for f in range(half, n_f...  13.3 us
    ppermute x4, waiting for transfers between devices, swap_front(): return lax.ppermute(x, 'front', [(f, f ^ mask) for f in range(count)])  10.8 us
    ppermute x3, starting transfers between devices, body(): sib = lax.ppermute(pk, leaf_bits[bits - level], [(0, 1), (1, 0)])  6.15 us
  transfers between devices with their start and end apart: 11, of which 2 were waited for; matrix products, arithmetic and copies ran while one was open for 6% of the time, Pallas kernels for 66%

profile of v1, /device:TPU:0, one launch (start us, length us, event | category | flops | bytes accessed | tf_op | source)
XLA Modules:
  0.0 297.3 jit_solution(8837304563178878759)
XLA Ops:
  7.2 0.8 convert_bitcast_fusion
  8.1 0.8 slice_bitcast_fusion
  11.0 0.8 convert_bitcast_fusion.1
  11.7 0.8 slice_bitcast_fusion.1
  13.2 1.3 fusion.2
  15.0 2.6 collective-permute-start
  17.6 1.3 collective-permute-start.3
  18.9 0.7 slice_bitcast_fusion.3
  19.6 0.7 convert_bitcast_fusion.2
  20.3 0.7 slice_bitcast_fusion.2
  21.0 10.8 %collective-permute-done = f32[256,512]{1,0:T(8,128)S(1)} collective-permute-done((f32[256,512]{1,0:T(8,128)S(1)}, f32[256,512]{1,0:T(8,128)S(1)}, u32[]{:S(2)}, u32[]{:S(2)}) %collective-permute-start) | collective-permute-done | bytes 524320 | tf_op jit(solution)/shard_map/ppermute | solution.py:370
  32.5 13.3 %collective-permute-done.3 = f32[256,512]{1,0:T(8,128)S(1)} collective-permute-done((f32[256,512]{1,0:T(8,128)S(1)}, f32[256,512]{1,0:T(8,128)S(1)}, u32[]{:S(2)}, u32[]{:S(2)}) %collective-permute-start.3) | collective-permute-done | bytes 524320 | tf_op jit(solution)/shard_map/ppermute | solution.py:400
  45.8 1.4 broadcast_select_fusion.4
  47.8 20.3 %head_factor.1 = (f32[512,512]{1,0:T(8,128)S(1)}, f32[512,128]{1,0:T(8,128)S(1)}, f32[8,128]{1,0:T(8,128)S(1)}) custom-call(f32[512,512]{1,0:T(8,128)S(1)} %get-tuple-element.25.head_ref), custom_call_target="tpu_custom_call" | custom-call | bytes 75000000 | tf_op jit(solution)/shard_map/head_factor/pallas_call | solution.py:322
  68.2 1.0 pad_maximum_fusion.2.tail_ref
  69.3 4.8 %leaf_update.1 = (f32[256,512]{1,0:T(8,128)S(1)}, f32[10,128,128]{2,1,0:T(8,128)S(1)}) custom-call(s32[2]{0:T(128)S(1)} %pad_add_fusion.pos_ref, f32[512,512]{1,0:T(8,128)S(1)} %get-tuple-element.13.fac_ref, f32[512,128]{1,0:T(8,128)S(1)} %get-tuple-element.14.x_ref, f32[8,128]{1,0:T(8,128)S(1)} %get-tuple-element.15.log_ref, ...), custom_call_target="tpu_custom_call" | custom-call | bytes 15000000 | tf_op jit(solution)/shard_map/leaf_update/pallas_call | solution.py:334
  74.1 1.9 collective-permute-start.5
  75.9 1.3 slice.74
  77.2 0.8 slice.75
  78.0 35.5 %densify.3 = f32[8192,128]{1,0:T(8,128)} custom-call(f32[1024,256]{1,0:T(8,128)S(1)} %bitcast.45), custom_call_target="tpu_custom_call" | custom-call | bytes 36000000 | tf_op jit(solution)/shard_map/densify/pallas_call | solution.py:309
  113.5 32.6 %level_front.3 = (f32[128,512]{1,0:T(8,128)S(1)}, f32[10,128,128]{2,1,0:T(8,128)S(1)}) custom-call(s32[2]{0:T(128)S(1)} %pad_add_fusion.pos_ref, f32[10,128,128]{2,1,0:T(8,128)S(1)} %get-tuple-element.17.own_pk, f32[10,128,128]{2,1,0:T(8,128)S(1)} %collective-permute-done.5.sib_pk, s32[14,512]{1,0:T(8,128)S(1)} %copy-done, f32[8,1024,128]{2,1,0:T(8,128)} %bitcast.51, ...), custom_call_target="tpu_custom_call" | custom-call | bytes 105000000 | tf_op jit(solution)/shard_map/level_front/pallas_call | solution.py:347
  146.1 1.6 collective-permute-start.6
  147.8 1.3 slice.76
  149.1 0.8 slice.77
  149.9 35.5 %densify.4 = f32[8192,128]{1,0:T(8,128)} custom-call(f32[1024,256]{1,0:T(8,128)S(1)} %bitcast.46), custom_call_target="tpu_custom_call" | custom-call | bytes 36000000 | tf_op jit(solution)/shard_map/densify/pallas_call | solution.py:309
  185.5 32.6 %level_front.4 = (f32[64,512]{1,0:T(8,128)S(1)}, f32[10,128,128]{2,1,0:T(8,128)S(1)}) custom-call(s32[2]{0:T(128)S(1)} %pad_add_fusion.pos_ref, f32[10,128,128]{2,1,0:T(8,128)S(1)} %get-tuple-element.19.own_pk, f32[10,128,128]{2,1,0:T(8,128)S(1)} %collective-permute-done.6.sib_pk, s32[14,512]{1,0:T(8,128)S(1)} %copy-done, f32[8,1024,128]{2,1,0:T(8,128)} %bitcast.50, ...), custom_call_target="tpu_custom_call" | custom-call | bytes 105000000 | tf_op jit(solution)/shard_map/level_front/pallas_call | solution.py:347
  218.1 2.7 collective-permute-start.7
  220.8 1.3 slice.78
  222.1 0.9 slice.79
  223.0 35.5 %densify.5 = f32[8192,128]{1,0:T(8,128)} custom-call(f32[1024,256]{1,0:T(8,128)S(1)} %bitcast.47), custom_call_target="tpu_custom_call" | custom-call | bytes 36000000 | tf_op jit(solution)/shard_map/densify/pallas_call | solution.py:309
  258.6 30.6 %level_front.5 = (f32[32,512]{1,0:T(8,128)S(1)}, f32[8,128]{1,0:T(8,128)S(1)}) custom-call(s32[2]{0:T(128)S(1)} %pad_add_fusion.pos_ref, f32[10,128,128]{2,1,0:T(8,128)S(1)} %get-tuple-element.21.own_pk, f32[10,128,128]{2,1,0:T(8,128)S(1)} %collective-permute-done.7.sib_pk, s32[14,512]{1,0:T(8,128)S(1)} %copy-done, f32[8,1024,128]{2,1,0:T(8,128)} %bitcast.49, ...), custom_call_target="tpu_custom_call" | custom-call | bytes 105000000 | tf_op jit(solution)/shard_map/level_front/pallas_call | solution.py:347
  289.8 1.0 maximum_bitcast_fusion
  (35 shorter events, 5.2 us)
Async XLA Ops:
  7.2 68.8 %all-gather.7.cloned.1.call-start = ((), (), s32[]{:S(2)}) async-start(), calls=%async_computation | async-start | bytes 1253376 | tf_op jit(solution)/shard_map/all_gather | solution.py:414
  10.3 137.5 %all-gather.9.cloned.1.call-start = ((), (), s32[]{:S(2)}) async-start(), calls=%async_computation.1 | async-start | bytes 1253376 | tf_op jit(solution)/shard_map/all_gather | solution.py:414
  13.2 207.6 %all-gather.11.cloned.1.call-start = ((), (), s32[]{:S(2)}) async-start(), calls=%async_computation.2 | async-start | bytes 1351680 | tf_op jit(solution)/shard_map/all_gather | solution.py:414
  14.5 18.0 %collective-permute-start.2 = (f32[256,512]{1,0:T(8,128)S(1)}, f32[256,512]{1,0:T(8,128)S(1)}, u32[]{:S(2)}, u32[]{:S(2)}) collective-permute-start(f32[256,512]{1,0:T(8,128)S(1)} %get-tuple-element.32), channel_id=1, source_target_pairs={{0,1},{1,0},{2,3},{3,2},{4,5},{5,4},{6,7},{7,6},{8,9},{9,8},{10,11... | collective-permute-start | bytes 1572872 | tf_op jit(solution)/shard_map/ppermute | solution.py:370
  15.0 16.8 %collective-permute-start = (f32[256,512]{1,0:T(8,128)S(1)}, f32[256,512]{1,0:T(8,128)S(1)}, u32[]{:S(2)}, u32[]{:S(2)}) collective-permute-start(f32[256,512]{1,0:T(8,128)S(1)} %get-tuple-element.32), channel_id=1, source_target_pairs={{0,2},{1,3},{2,0},{3,1},{4,6},{5,7},{6,4},{7,5},{8,10},{9,11},{10,... | collective-permute-start | bytes 1572872 | tf_op jit(solution)/shard_map/ppermute | solution.py:370
  17.6 28.2 %collective-permute-start.3 = (f32[256,512]{1,0:T(8,128)S(1)}, f32[256,512]{1,0:T(8,128)S(1)}, u32[]{:S(2)}, u32[]{:S(2)}) collective-permute-start(f32[256,512]{1,0:T(8,128)S(1)} %get-tuple-element.31), channel_id=1, source_target_pairs={{2,0},{3,1},{6,4},{7,5},{10,8},{11,9},{14,12},{15,13},{18,16},{19,... | collective-permute-start | bytes 1572872 | tf_op jit(solution)/shard_map/ppermute | solution.py:400
  31.8 15.6 %collective-permute-start.1 = (f32[256,512]{1,0:T(8,128)S(1)}, f32[256,512]{1,0:T(8,128)S(1)}, u32[]{:S(2)}, u32[]{:S(2)}) collective-permute-start(f32[256,512]{1,0:T(8,128)S(1)} %collective-permute-done), channel_id=1, source_target_pairs={{0,1},{1,0},{2,3},{3,2},{4,5},{5,4},{6,7},{7,6},{8,9},{9,8},{10,11... | collective-permute-start | bytes 1572872 | tf_op jit(solution)/shard_map/ppermute | solution.py:370
  47.2 20.9 %collective-permute-start.4 = (f32[256,512]{1,0:T(8,128)S(1)}, f32[256,512]{1,0:T(8,128)S(1)}, u32[]{:S(2)}, u32[]{:S(2)}) collective-permute-start(f32[256,512]{1,0:T(8,128)S(1)} %get-tuple-element.30), channel_id=1, source_target_pairs={{0,1},{1,0},{2,3},{3,2},{4,5},{5,4},{6,7},{7,6},{8,9},{9,8},{10,11... | collective-permute-start | bytes 1572872 | tf_op jit(solution)/shard_map/ppermute | solution.py:370
  74.1 39.4 %copy-start = (s32[14,512]{1,0:T(8,128)S(1)}, s32[14,512]{1,0:T(8,128)}, u32[]{:S(2)}) copy-start(s32[14,512]{1,0:T(8,128)} %maps_ref.5) | copy-start | bytes 86020
  74.1 39.4 %collective-permute-start.5 = (f32[10,128,128]{2,1,0:T(8,128)S(1)}, f32[10,128,128]{2,1,0:T(8,128)S(1)}, u32[]{:S(2)}, u32[]{:S(2)}) collective-permute-start(f32[10,128,128]{2,1,0:T(8,128)S(1)} %get-tuple-element.17.own_pk), channel_id=1, source_target_pairs={{0,4},{4,0},{1,5},{5,1},{2,6},{6,2},{3,7},{7,3},{8,12},{12,8},{9,1... | collective-permute-start | bytes 1966088 | tf_op jit(solution)/shard_map/ppermute | solution.py:425
  146.1 39.4 %collective-permute-start.6 = (f32[10,128,128]{2,1,0:T(8,128)S(1)}, f32[10,128,128]{2,1,0:T(8,128)S(1)}, u32[]{:S(2)}, u32[]{:S(2)}) collective-permute-start(f32[10,128,128]{2,1,0:T(8,128)S(1)} %get-tuple-element.19.own_pk), channel_id=1, source_target_pairs={{0,8},{8,0},{1,9},{9,1},{2,10},{10,2},{3,11},{11,3},{4,12},{12,4},... | collective-permute-start | bytes 1966088 | tf_op jit(solution)/shard_map/ppermute | solution.py:425
  218.1 40.5 %collective-permute-start.7 = (f32[10,128,128]{2,1,0:T(8,128)S(1)}, f32[10,128,128]{2,1,0:T(8,128)S(1)}, u32[]{:S(2)}, u32[]{:S(2)}) collective-permute-start(f32[10,128,128]{2,1,0:T(8,128)S(1)} %get-tuple-element.21.own_pk), channel_id=1, source_target_pairs={{0,16},{16,0},{1,17},{17,1},{2,18},{18,2},{3,19},{19,3},{4,20},{20... | collective-permute-start | bytes 1966088 | tf_op jit(solution)/shard_map/ppermute | solution.py:425
Sparse Core Ops, SparseCore 0:
  10.5 31.0 all-gather.6
  43.2 30.1 all-gather.8
  76.2 53.7 all-gather.10
